TPU v7x, 512 devices: a whole 4x4x16 slice. The times are simulated.
512 devices in a mesh: expert: 128 (over y, z, core), half: 4 (over x).
Axes of the slice: x: 4, y: 4, z: 16, core: 2. Of those that a mesh axis runs over, the one named last changes fastest.
Arguments:
- tokens: bfloat16 [2048, 2048], P('expert', 'half'), may hold values from -6 to 6
- upstream: bfloat16 [2048, 2048], P('expert', 'half'), may hold values from -6 to 6
- expert_ids: int32 [2048, 8], P('expert'), may hold values from 0 to 127, all different within a row; in each aligned block of 16 rows (0 to 15, 16 to 31, ...) at most 2 rows name the same one
- gate_probs: float32 [2048, 8], P('expert'), may hold values from 0.01 to 1
- pad_mask: int32 [2048], P('expert'), may hold values 0 or 1
- gate_weight: bfloat16 [128, 2048, 1536], P('expert', None, 'half'), may hold values from -0.125 to 0.125
- up_weight: bfloat16 [128, 2048, 1536], P('expert', None, 'half'), may hold values from -0.125 to 0.125
- down_weight: bfloat16 [128, 1536, 2048], P('expert', 'half'), may hold values from -0.15625 to 0.15625
Outputs:
- layer_out: bfloat16 [2048, 2048], P('expert', 'half')
- grad_tokens: bfloat16 [2048, 2048], P('expert', 'half')
Inputs may be any that keep to these rules, and one draw needn't show every extreme that they name: `expert_ids`: each row names 8 different experts. In the rows of one device (aligned blocks of 16 rows) no expert is named more than 2 times, a bound that some block reaches.
All inputs are finite; a program needn't handle non-finite values. No bound on the sum of `pad_mask` on one device may be relied on, other than what follows from the above.
Results may differ from a plain program's by a relative error of at most 0.025.
Values may be sent and summed in bfloat16 or wider, within the bound.
No kernel may reach another device: no remote copies, remote signals or barrier semaphores. Data moves between devices by JAX's collectives and lax.ppermute only.
A program may use at most 64 MiB of HBM per device.

v0:
```python
import math
import jax
import jax.numpy as jnp
from jax import lax
from jax.sharding import PartitionSpec as P

orth_weight = 0.25


def assign_slots(expert_ids, experts, capacity):
    tok_count, top_count = expert_ids.shape
    flat_ids = expert_ids.reshape(tok_count * top_count)
    onehot = (flat_ids[:, None] == jnp.arange(experts, dtype=jnp.int32)[None, :]).astype(jnp.int32)
    before = jnp.cumsum(onehot, axis=0) - onehot
    slot_index = jnp.sum(before * onehot, axis=1)
    return flat_ids * capacity + slot_index


def placement_matrix(slot_dest, slots_total):
    row_index = jnp.arange(slots_total, dtype=jnp.int32)
    return (row_index[:, None] == slot_dest[None, :]).astype(jnp.bfloat16)


def to_experts(place, items):
    whole = lax.all_gather(items, "half", axis=1, tiled=True)
    buckets = jnp.dot(place, whole, preferred_element_type=jnp.float32).astype(jnp.bfloat16)
    return lax.all_to_all(buckets, "expert", split_axis=0, concat_axis=0, tiled=True)


def to_homes(partial_value):
    summed = lax.psum_scatter(
        partial_value.astype(jnp.bfloat16), "half", scatter_dimension=1, tiled=True
    )
    return lax.all_to_all(summed, "expert", split_axis=0, concat_axis=0, tiled=True)


def shards(tokens, upstream, expert_ids, gate_probs, pad_mask, gate_weight, up_weight, down_weight):
    tok_count, top_count = expert_ids.shape
    experts = lax.axis_size("expert")
    capacity = min(tok_count, 2 * tok_count * top_count // experts)
    slots_total = experts * capacity
    full_width = tokens.shape[1] * lax.axis_size("half")
    slot_dest = assign_slots(expert_ids, experts, capacity)
    place_items = placement_matrix(slot_dest, slots_total)
    place_tokens = jnp.sum(place_items.reshape(slots_total, tok_count, top_count), axis=2)
    weight_gate = gate_weight[0]
    weight_up = up_weight[0]
    weight_down = down_weight[0]
    rows_in = to_experts(place_tokens, tokens)
    gate_val = jnp.dot(rows_in, weight_gate, preferred_element_type=jnp.float32)
    up_val = jnp.dot(rows_in, weight_up, preferred_element_type=jnp.float32)
    hidden_act = (jax.nn.silu(gate_val) * up_val).astype(jnp.bfloat16)
    partial_value = jnp.dot(hidden_act, weight_down, preferred_element_type=jnp.float32)
    out_home = to_homes(partial_value)
    outputs = jnp.take(out_home, slot_dest, axis=0).reshape(tok_count, top_count, -1)
    out_float = outputs.astype(jnp.float32)
    shares = gate_probs / jnp.sum(gate_probs, axis=1, keepdims=True)
    layer_out = jnp.sum(shares[:, :, None] * out_float, axis=1).astype(jnp.bfloat16)
    gram_part = jnp.einsum("tjd,tkd->tjk", out_float, out_float) / math.sqrt(full_width)
    gram = lax.psum(gram_part, "half")
    off_diag = 1.0 - jnp.eye(top_count, dtype=jnp.float32)
    coeffs = orth_weight * gram * off_diag
    grad_out = pad_mask.astype(jnp.float32)[:, None, None] * (
        shares[:, :, None] * upstream.astype(jnp.float32)[:, None, :]
        + jnp.einsum("tjk,tkd->tjd", coeffs, out_float)
    )
    grad_items = grad_out.astype(jnp.bfloat16).reshape(tok_count * top_count, -1)
    grad_rows = to_experts(place_items, grad_items)
    grad_act = jnp.einsum("rd,hd->rh", grad_rows, weight_down, preferred_element_type=jnp.float32)
    sigma = jax.nn.sigmoid(gate_val)
    grad_gate = (grad_act * up_val * sigma * (1.0 + gate_val * (1.0 - sigma))).astype(jnp.bfloat16)
    grad_up = (grad_act * gate_val * sigma).astype(jnp.bfloat16)
    grad_partial = jnp.einsum(
        "rh,dh->rd", grad_gate, weight_gate, preferred_element_type=jnp.float32
    )
    grad_partial = grad_partial + jnp.einsum(
        "rh,dh->rd", grad_up, weight_up, preferred_element_type=jnp.float32
    )
    grad_home = to_homes(grad_partial)
    grad_pairs = jnp.take(grad_home, slot_dest, axis=0).reshape(tok_count, top_count, -1)
    grad_tokens = jnp.sum(grad_pairs.astype(jnp.float32), axis=1).astype(jnp.bfloat16)
    return (layer_out, grad_tokens)


def solution(mesh):
    in_specs = (
        P("expert", "half"),
        P("expert", "half"),
        P("expert", None),
        P("expert", None),
        P("expert"),
        P("expert", None, "half"),
        P("expert", None, "half"),
        P("expert", "half", None),
    )
    out_specs = (P("expert", "half"), P("expert", "half"))
    return jax.shard_map(shards, mesh=mesh, in_specs=in_specs, out_specs=out_specs, check_vma=False)
```

profile of v0, /device:TPU:1, one launch (start us, length us, event | category | flops | bytes accessed | tf_op | source)
XLA Modules:
  0.0 342.9 jit_solution(6629864669466501402)
XLA Ops:
  7.2 0.9 copy.17
  8.9 10.4 %all_gather.6 = bf16[16,2048]{1,0:T(8,128)(2,1)S(1)} all-gather(bf16[16,512]{1,0:T(8,128)(2,1)} %param.10), channel_id=1, replica_groups=mesh['expert'=128,'half'=4] {'half'}, dimensions={1}, use_global_device_ids=true | all-gather | bytes 81920 | tf_op jit(solution)/shard_map/all_gather | solution.py:25
  19.7 1.5 all_to_all.32
  21.2 77.1 %all_to_all.48 = bf16[128,2,2048]{2,1,0:T(2,128)(2,1)} all-to-all(bf16[128,2,2048]{2,1,0:T(2,128)(2,1)} %all_to_all.32), channel_id=1, replica_groups=mesh['expert'=128,'half'=4] {'expert'}, dimensions={0} | all-to-all | bytes 2097152 | tf_op jit(solution)/shard_map/all_to_all | solution.py:27
  98.3 1.5 all_to_all.34
  99.8 2.2 fusion.9
  102.7 1.7 convolution_convert_fusion.1
  104.5 22.2 %reduce-scatter.3.cloned.1.call-done = bf16[256,512]{1,0:T(8,128)(2,1)} async-done(((bf16[256,2048]{1,0:T(8,128)(2,1)}), bf16[256,512]{1,0:T(8,128)(2,1)}) %reduce-scatter.3.cloned.1.call-update) | async-done | bytes 262160 | tf_op jit(solution)/shard_map/reduce_scatter | solution.py:31
  126.7 1.7 all_to_all.35
  128.4 18.4 %all-to-all-start.1 = ((bf16[128,2,512]{2,1,0:T(2,128)(2,1)}), bf16[128,2,512]{2,1,0:T(2,128)(2,1)S(1)}, u32[]{:S(2)}, u32[]{:S(2)}) async-start(bf16[128,2,512]{2,1,0:T(2,128)(2,1)} %all_to_all.35), calls=%async_computation.2 | async-start | bytes 524288 | tf_op jit(solution)/shard_map/all_to_all | solution.py:34
  147.1 22.2 %all-to-all-done.1 = bf16[128,2,512]{2,1,0:T(2,128)(2,1)S(1)} async-done(((bf16[128,2,512]{2,1,0:T(2,128)(2,1)}), bf16[128,2,512]{2,1,0:T(2,128)(2,1)S(1)}, u32[]{:S(2)}, u32[]{:S(2)}) %all-to-all-start.1) | async-done | bytes 262176 | tf_op jit(solution)/shard_map/all_to_all | solution.py:34
  169.4 0.8 gather_fusion
  170.5 11.8 %psum.7 = f32[16,8,8]{2,1,0:T(8,128)S(1)} all-reduce(f32[16,8,8]{2,1,0:T(8,128)S(1)} %convolution_multiply_fusion), channel_id=1, replica_groups=mesh['expert'=128,'half'=4] {'half'}, use_global_device_ids=true, to_apply=%region_6.8 | all-reduce | flops 1024 | bytes 8192 | tf_op jit(solution)/shard_map/psum | solution.py:60
  182.6 10.1 %all_gather.7 = bf16[128,2048]{1,0:T(8,128)(2,1)S(1)} all-gather(bf16[128,512]{1,0:T(8,128)(2,1)S(1)} %fusion.13), channel_id=1, replica_groups=mesh['expert'=128,'half'=4] {'half'}, dimensions={1}, use_global_device_ids=true | all-gather | bytes 655360 | tf_op jit(solution)/shard_map/all_gather | solution.py:25
  192.7 1.1 convolution_convert_fusion
  193.8 1.5 all_to_all.38
  195.3 69.1 %all_to_all.49 = bf16[128,2,2048]{2,1,0:T(2,128)(2,1)} all-to-all(bf16[128,2,2048]{2,1,0:T(2,128)(2,1)} %all_to_all.38), channel_id=1, replica_groups=mesh['expert'=128,'half'=4] {'expert'}, dimensions={0} | all-to-all | bytes 2097152 | tf_op jit(solution)/shard_map/all_to_all | solution.py:27
  264.4 1.5 all_to_all.40
  268.7 1.8 fusion
  270.5 20.9 %reduce-scatter.5.cloned.1.call-done = bf16[256,512]{1,0:T(8,128)(2,1)} async-done(((bf16[256,2048]{1,0:T(8,128)(2,1)}), bf16[256,512]{1,0:T(8,128)(2,1)}) %reduce-scatter.5.cloned.1.call-update) | async-done | bytes 262160 | tf_op jit(solution)/shard_map/reduce_scatter | solution.py:31
  291.4 1.7 all_to_all.41
  293.2 18.7 %all-to-all-start.3 = ((bf16[128,2,512]{2,1,0:T(2,128)(2,1)}), bf16[128,2,512]{2,1,0:T(2,128)(2,1)S(1)}, u32[]{:S(2)}, u32[]{:S(2)}) async-start(bf16[128,2,512]{2,1,0:T(2,128)(2,1)} %all_to_all.41), calls=%async_computation.5 | async-start | bytes 524288 | tf_op jit(solution)/shard_map/all_to_all | solution.py:34
  312.6 21.7 %all-to-all-done.3 = bf16[128,2,512]{2,1,0:T(2,128)(2,1)S(1)} async-done(((bf16[128,2,512]{2,1,0:T(2,128)(2,1)}), bf16[128,2,512]{2,1,0:T(2,128)(2,1)S(1)}, u32[]{:S(2)}, u32[]{:S(2)}) %all-to-all-start.3) | async-done | bytes 262176 | tf_op jit(solution)/shard_map/all_to_all | solution.py:34
  334.5 0.8 gather_fusion.1
  (46 shorter events, 7.2 us)
Async XLA Ops:
  7.2 95.6 %copy-start = (bf16[1,384,2048]{2,1,0:T(8,128)(2,1)S(1)}, bf16[1,384,2048]{2,1,0:T(8,128)(2,1)}, u32[]{:S(2)}) copy-start(bf16[1,384,2048]{2,1,0:T(8,128)(2,1)} %param.17) | copy-start | bytes 4718596
  7.2 119.5 %reduce-scatter.3.cloned.1.call-start = ((), (), s32[]{:S(2)}) async-start(), calls=%async_computation.6 | async-start | bytes 1310720 | tf_op jit(solution)/shard_map/reduce_scatter | solution.py:31
  99.8 2.2 copy-start.2
  104.5 42.4 %copy-start.7 = (s32[16]{0:T(128)S(1)}, s32[16]{0:T(128)}, u32[]{:S(2)}) copy-start(s32[16]{0:T(128)} %param.14) | copy-start | bytes 196
  104.5 42.4 %copy-start.5 = (f32[16,8]{0,1:T(8,128)S(1)}, f32[16,8]{0,1:T(8,128)}, u32[]{:S(2)}) copy-start(f32[16,8]{0,1:T(8,128)} %param.13) | copy-start | bytes 1540
  104.5 42.5 %copy-start.4 = (bf16[16,512]{1,0:T(8,128)(2,1)S(1)}, bf16[16,512]{1,0:T(8,128)(2,1)}, u32[]{:S(2)}) copy-start(bf16[16,512]{1,0:T(8,128)(2,1)} %param.11) | copy-start | bytes 49156
  128.4 40.9 %all-to-all-start.1 = ((bf16[128,2,512]{2,1,0:T(2,128)(2,1)}), bf16[128,2,512]{2,1,0:T(2,128)(2,1)S(1)}, u32[]{:S(2)}, u32[]{:S(2)}) async-start(bf16[128,2,512]{2,1,0:T(2,128)(2,1)} %all_to_all.35), calls=%async_computation.2 | async-start | bytes 524288 | tf_op jit(solution)/shard_map/all_to_all | solution.py:34
  146.8 144.6 %reduce-scatter.5.cloned.1.call-start = ((), (), s32[]{:S(2)}) async-start(), calls=%async_computation.7 | async-start | bytes 1310720 | tf_op jit(solution)/shard_map/reduce_scatter | solution.py:31
  147.0 22.3 %copy-start.6 = (s32[128]{0:T(128)}, s32[128]{0:T(128)S(1)}, u32[]{:S(2)}) copy-start(s32[128]{0:T(128)S(1)} %get-tuple-element.4) | copy-start | bytes 1540
  265.9 1.4 copy-start.1
  267.3 1.4 copy-start.3
  293.2 41.2 %all-to-all-start.3 = ((bf16[128,2,512]{2,1,0:T(2,128)(2,1)}), bf16[128,2,512]{2,1,0:T(2,128)(2,1)S(1)}, u32[]{:S(2)}, u32[]{:S(2)}) async-start(bf16[128,2,512]{2,1,0:T(2,128)(2,1)} %all_to_all.41), calls=%async_computation.5 | async-start | bytes 524288 | tf_op jit(solution)/shard_map/all_to_all | solution.py:34
Sparse Core Ops, SparseCore 0:
  104.6 22.0 reduce-scatter.2
  270.6 20.7 reduce-scatter.4
where the time goes:
time: 344 us; the launch traced here: 343 us
  blocking collectives  178 us (52%)
  waiting for transfers between devices  87.1 us (25%)
  starting transfers between devices  37.2 us (11%)
  between operations  14.3 us (4%)
  local copies, waits for them, and re-layouts  13.8 us (4%)
  matrix products  9.94 us (3%)
    all_to_all x2, blocking collectives, to_experts(): lax.all_to_all(buckets, 'expert', split_axis=0, concat_axis=0, tiled=True)  146 us
    all_to_all x2, waiting for transfers between devices, to_homes(): lax.all_to_all(summed, 'expert', split_axis=0, concat_axis=0, tiled=True)  44 us
    reduce_scatter x2, waiting for transfers between devices, to_homes(): lax.psum_scatter(partial_value.astype(jnp.bfloat16), 'half', scatter_dime...  43.1 us
    all_to_all x2, starting transfers between devices, to_homes(): lax.all_to_all(summed, 'expert', split_axis=0, concat_axis=0, tiled=True)  37.1 us
    all_gather x2, blocking collectives, to_experts(): whole = lax.all_gather(items, 'half', axis=1, tiled=True)  20.5 us
    psum x1, blocking collectives, shards(): gram = lax.psum(gram_part, 'half')  11.8 us
  transfers between devices with their start and end apart: 4, of which 4 were waited for; matrix products, arithmetic and copies ran while one was open for 0% of the time, Pallas kernels for 0%

commit v1 on v0

--- a/solution.py
+++ b/solution.py
@@ -57,7 +57,9 @@
     shares = gate_probs / jnp.sum(gate_probs, axis=1, keepdims=True)
     layer_out = jnp.sum(shares[:, :, None] * out_float, axis=1).astype(jnp.bfloat16)
     gram_part = jnp.einsum("tjd,tkd->tjk", out_float, out_float) / math.sqrt(full_width)
-    gram = lax.psum(gram_part, "half")
+    gram = gram_part
+    for hop in (1, 2):
+        gram = gram + lax.ppermute(gram, "half", [(dev, dev ^ hop) for dev in range(4)])
     off_diag = 1.0 - jnp.eye(top_count, dtype=jnp.float32)
     coeffs = orth_weight * gram * off_diag
     grad_out = pad_mask.astype(jnp.float32)[:, None, None] * (

time: 344 us -> 343 us (level)
  blocking collectives: 178 us -> 166 us
  waiting for transfers between devices: 87.1 us -> 93.2 us
  starting transfers between devices: 37.2 us -> 42.5 us
    psum x1 -> x0, blocking collectives: 11.8 us -> none  [shards(): gram = lax.psum(gram_part, 'half')]
    ppermute x0 -> x2, waiting for transfers between devices: none -> 6.37 us  [shards(): lax.ppermute(gram, 'half', [(dev, dev ^ hop) for dev in range(4)])]
    ppermute x0 -> x2, starting transfers between devices: none -> 5.01 us  [shards(): lax.ppermute(gram, 'half', [(dev, dev ^ hop) for dev in range(4)])]
  transfers between devices with their start and end apart: 4 -> 6, of which waited for: 4 -> 6; matrix products, arithmetic and copies ran while one was open for 0% -> 0% of each run, Pallas kernels for 0% -> 0%
where the time goes in v1:
time: 343 us; the launch traced here: 342 us
  blocking collectives  166 us (48%)
  waiting for transfers between devices  93.2 us (27%)
  starting transfers between devices  42.5 us (12%)
  between operations  14.3 us (4%)
  local copies, waits for them, and re-layouts  13.8 us (4%)
  matrix products  9.93 us (3%)
    all_to_all x2, blocking collectives, to_experts(): lax.all_to_all(buckets, 'expert', split_axis=0, concat_axis=0, tiled=True)  145 us
    all_to_all x2, waiting for transfers between devices, to_homes(): lax.all_to_all(summed, 'expert', split_axis=0, concat_axis=0, tiled=True)  44.1 us
    reduce_scatter x2, waiting for transfers between devices, to_homes(): lax.psum_scatter(partial_value.astype(jnp.bfloat16), 'half', scatter_dime...  42.7 us
    all_to_all x2, starting transfers between devices, to_homes(): lax.all_to_all(summed, 'expert', split_axis=0, concat_axis=0, tiled=True)  37.4 us
    all_gather x2, blocking collectives, to_experts(): whole = lax.all_gather(items, 'half', axis=1, tiled=True)  21.1 us
  transfers between devices with their start and end apart: 6, of which 6 were waited for; matrix products, arithmetic and copies ran while one was open for 0% of the time, Pallas kernels for 0%

profile of v1, /device:TPU:1, one launch (start us, length us, event | category | flops | bytes accessed | tf_op | source)
XLA Modules:
  0.0 341.9 jit_solution(7083271647533160061)
XLA Ops:
  8.9 10.4 %all_gather.6 = bf16[16,2048]{1,0:T(8,128)(2,1)S(1)} all-gather(bf16[16,512]{1,0:T(8,128)(2,1)} %param.10), channel_id=1, replica_groups=mesh['expert'=128,'half'=4] {'half'}, dimensions={1}, use_global_device_ids=true | all-gather | bytes 81920 | tf_op jit(solution)/shard_map/all_gather | solution.py:25
  19.7 1.5 all_to_all.32
  21.2 77.1 %all_to_all.48 = bf16[128,2,2048]{2,1,0:T(2,128)(2,1)} all-to-all(bf16[128,2,2048]{2,1,0:T(2,128)(2,1)} %all_to_all.32), channel_id=1, replica_groups=mesh['expert'=128,'half'=4] {'expert'}, dimensions={0} | all-to-all | bytes 2097152 | tf_op jit(solution)/shard_map/all_to_all | solution.py:27
  98.3 1.5 all_to_all.34
  99.8 2.2 fusion.9
  102.7 1.7 convolution_convert_fusion.1
  104.5 21.8 %reduce-scatter.3.cloned.1.call-done = bf16[256,512]{1,0:T(8,128)(2,1)} async-done(((bf16[256,2048]{1,0:T(8,128)(2,1)}), bf16[256,512]{1,0:T(8,128)(2,1)}) %reduce-scatter.3.cloned.1.call-update) | async-done | bytes 262160 | tf_op jit(solution)/shard_map/reduce_scatter | solution.py:31
  126.3 1.7 all_to_all.35
  128.1 18.7 %all-to-all-start.1 = ((bf16[128,2,512]{2,1,0:T(2,128)(2,1)}), bf16[128,2,512]{2,1,0:T(2,128)(2,1)S(1)}, u32[]{:S(2)}, u32[]{:S(2)}) async-start(bf16[128,2,512]{2,1,0:T(2,128)(2,1)} %all_to_all.35), calls=%async_computation.2 | async-start | bytes 524288 | tf_op jit(solution)/shard_map/all_to_all | solution.py:34
  146.9 22.4 %all-to-all-done.1 = bf16[128,2,512]{2,1,0:T(2,128)(2,1)S(1)} async-done(((bf16[128,2,512]{2,1,0:T(2,128)(2,1)}), bf16[128,2,512]{2,1,0:T(2,128)(2,1)S(1)}, u32[]{:S(2)}, u32[]{:S(2)}) %all-to-all-start.1) | async-done | bytes 262176 | tf_op jit(solution)/shard_map/all_to_all | solution.py:34
  170.5 1.9 collective-permute-start
  172.4 3.1 collective-permute-done
  175.5 3.1 collective-permute-start.1
  178.7 3.3 collective-permute-done.1
  182.3 10.8 %all_gather.7 = bf16[128,2048]{1,0:T(8,128)(2,1)S(1)} all-gather(bf16[128,512]{1,0:T(8,128)(2,1)S(1)} %fusion.13), channel_id=1, replica_groups=mesh['expert'=128,'half'=4] {'half'}, dimensions={1}, use_global_device_ids=true | all-gather | bytes 655360 | tf_op jit(solution)/shard_map/all_gather | solution.py:25
  193.1 1.1 convolution_convert_fusion
  194.2 1.5 all_to_all.38
  195.7 67.7 %all_to_all.49 = bf16[128,2,2048]{2,1,0:T(2,128)(2,1)} all-to-all(bf16[128,2,2048]{2,1,0:T(2,128)(2,1)} %all_to_all.38), channel_id=1, replica_groups=mesh['expert'=128,'half'=4] {'expert'}, dimensions={0} | all-to-all | bytes 2097152 | tf_op jit(solution)/shard_map/all_to_all | solution.py:27
  263.4 1.5 all_to_all.40
  267.7 1.8 fusion
  269.5 20.9 %reduce-scatter.5.cloned.1.call-done = bf16[256,512]{1,0:T(8,128)(2,1)} async-done(((bf16[256,2048]{1,0:T(8,128)(2,1)}), bf16[256,512]{1,0:T(8,128)(2,1)}) %reduce-scatter.5.cloned.1.call-update) | async-done | bytes 262160 | tf_op jit(solution)/shard_map/reduce_scatter | solution.py:31
  290.4 1.7 all_to_all.41
  292.1 18.7 %all-to-all-start.3 = ((bf16[128,2,512]{2,1,0:T(2,128)(2,1)}), bf16[128,2,512]{2,1,0:T(2,128)(2,1)S(1)}, u32[]{:S(2)}, u32[]{:S(2)}) async-start(bf16[128,2,512]{2,1,0:T(2,128)(2,1)} %all_to_all.41), calls=%async_computation.5 | async-start | bytes 524288 | tf_op jit(solution)/shard_map/all_to_all | solution.py:34
  311.6 21.7 %all-to-all-done.3 = bf16[128,2,512]{2,1,0:T(2,128)(2,1)S(1)} async-done(((bf16[128,2,512]{2,1,0:T(2,128)(2,1)}), bf16[128,2,512]{2,1,0:T(2,128)(2,1)S(1)}, u32[]{:S(2)}, u32[]{:S(2)}) %all-to-all-start.3) | async-done | bytes 262176 | tf_op jit(solution)/shard_map/all_to_all | solution.py:34
  (50 shorter events, 9.7 us)
Async XLA Ops:
  7.2 95.6 %copy-start = (bf16[1,384,2048]{2,1,0:T(8,128)(2,1)S(1)}, bf16[1,384,2048]{2,1,0:T(8,128)(2,1)}, u32[]{:S(2)}) copy-start(bf16[1,384,2048]{2,1,0:T(8,128)(2,1)} %param.17) | copy-start | bytes 4718596
  7.2 119.1 %reduce-scatter.3.cloned.1.call-start = ((), (), s32[]{:S(2)}) async-start(), calls=%async_computation.6 | async-start | bytes 1310720 | tf_op jit(solution)/shard_map/reduce_scatter | solution.py:31
  99.7 2.2 copy-start.2
  104.4 42.4 %copy-start.5 = (f32[16,8]{0,1:T(8,128)S(1)}, f32[16,8]{0,1:T(8,128)}, u32[]{:S(2)}) copy-start(f32[16,8]{0,1:T(8,128)} %param.13) | copy-start | bytes 1540
  104.5 74.2 %copy-start.7 = (s32[16]{0:T(128)S(1)}, s32[16]{0:T(128)}, u32[]{:S(2)}) copy-start(s32[16]{0:T(128)} %param.14) | copy-start | bytes 196
  104.5 74.3 %copy-start.4 = (bf16[16,512]{1,0:T(8,128)(2,1)S(1)}, bf16[16,512]{1,0:T(8,128)(2,1)}, u32[]{:S(2)}) copy-start(bf16[16,512]{1,0:T(8,128)(2,1)} %param.11) | copy-start | bytes 49156
  128.1 41.2 %all-to-all-start.1 = ((bf16[128,2,512]{2,1,0:T(2,128)(2,1)}), bf16[128,2,512]{2,1,0:T(2,128)(2,1)S(1)}, u32[]{:S(2)}, u32[]{:S(2)}) async-start(bf16[128,2,512]{2,1,0:T(2,128)(2,1)} %all_to_all.35), calls=%async_computation.2 | async-start | bytes 524288 | tf_op jit(solution)/shard_map/all_to_all | solution.py:34
  146.8 143.6 %reduce-scatter.5.cloned.1.call-start = ((), (), s32[]{:S(2)}) async-start(), calls=%async_computation.7 | async-start | bytes 1310720 | tf_op jit(solution)/shard_map/reduce_scatter | solution.py:31
  146.9 22.4 %copy-start.6 = (s32[128]{0:T(128)}, s32[128]{0:T(128)S(1)}, u32[]{:S(2)}) copy-start(s32[128]{0:T(128)S(1)} %get-tuple-element.4) | copy-start | bytes 1540
  170.5 5.0 %collective-permute-start = (f32[16,8,8]{2,1,0:T(8,128)S(1)}, f32[16,8,8]{2,1,0:T(8,128)S(1)}, u32[]{:S(2)}, u32[]{:S(2)}) collective-permute-start(f32[16,8,8]{2,1,0:T(8,128)S(1)} %convolution_multiply_fusion), channel_id=1, source_target_pairs={{0,1},{1,0},{2,3},{3,2},{4,5},{5,4},{6,7},{7,6},{8,9},{9,8},{10,11... | collective-permute-start | bytes 12296 | tf_op jit(solution)/shard_map/ppermute | solution.py:62
  175.5 6.5 %collective-permute-start.1 = (f32[16,8,8]{2,1,0:T(8,128)S(1)}, f32[16,8,8]{2,1,0:T(8,128)S(1)}, u32[]{:S(2)}, u32[]{:S(2)}) collective-permute-start(f32[16,8,8]{2,1,0:T(8,128)S(1)} %add.43), channel_id=1, source_target_pairs={{0,2},{1,3},{2,0},{3,1},{4,6},{5,7},{6,4},{7,5},{8,10},{9,11},{10,... | collective-permute-start | bytes 12296 | tf_op jit(solution)/shard_map/ppermute | solution.py:62
  264.9 1.4 copy-start.1
  266.3 1.4 copy-start.3
  292.1 41.2 %all-to-all-start.3 = ((bf16[128,2,512]{2,1,0:T(2,128)(2,1)}), bf16[128,2,512]{2,1,0:T(2,128)(2,1)S(1)}, u32[]{:S(2)}, u32[]{:S(2)}) async-start(bf16[128,2,512]{2,1,0:T(2,128)(2,1)} %all_to_all.41), calls=%async_computation.5 | async-start | bytes 524288 | tf_op jit(solution)/shard_map/all_to_all | solution.py:34
Sparse Core Ops, SparseCore 0:
  104.6 21.6 reduce-scatter.2
  269.6 20.7 reduce-scatter.4
